TPU v7x, 512 devices: a whole 4x4x16 slice. The times are simulated.
512 devices in a mesh: slab: 16 (over z_lo, y), rcv: 32 (over x, z_hi, core).
Axes of the slice: x: 4, y: 4, z: 16 (z_hi: 4, z_lo: 4; z = z_hi * 4 + z_lo), core: 2. Of those that a mesh axis runs over, the one named last changes fastest.
Arguments:
- adjoint_now: float32 [32, 64, 128, 128], P('rcv', 'slab'), may hold values from -6 to 6
- adjoint_before: float32 [32, 64, 128, 128], P('rcv', 'slab'), may hold values from -6 to 6
- courant_field: float32 [64, 128, 128], P('slab'), may hold values from 0.04 to 0.2
- log_buoyancy: float32 [64, 128, 128], P('slab'), may hold values from -0.3 to 0.3
- snapshot_store: float32 [32, 64, 128, 128], P('rcv', 'slab'), may hold values from -6 to 6
- owner_order: int32 [32], replicated, may hold values from 0 to 31, each once
- receiver_cells: int32 [32], P('rcv'), may hold values from 0 to 1048575
- receiver_traces: float32 [32, 8], P('rcv'), may hold values from -6 to 6
- residual_weights: float32 [32], P('rcv'), may hold values from -0.3 to 0.3
Outputs:
- sensitivity: float32 [64, 128, 128], P('slab', 'rcv')
- adjoint_after: float32 [32, 64, 128, 128], P('rcv', 'slab')
Inputs may be any that keep to these rules, and one draw needn't show every extreme that they name: Each slot number appears once; checkpoint k reads slot owner_order[k] for k < 4. `receiver_cells`: a cell of the grid.
All inputs are finite; a program needn't handle non-finite values.
Results may differ from a plain program's by a relative error of at most 0.0003.
Values sent between devices are 32-bit elements; how exact they have to be, the bound alone decides.
A program may use at most 64 MiB of HBM per device.

v0:
```python
import jax
import jax.numpy as jnp
from jax import lax
from jax.sharding import PartitionSpec as P

SNAPS = 4


def extended(shard, sides, width):
    for axis, dim in sides:
        peers, length = (lax.axis_size(axis), shard.shape[dim])
        up = [(i, (i + 1) % peers) for i in range(peers - 1)]
        down = [(j, i) for i, j in up]
        last = lax.slice_in_dim(shard, length - width, length, axis=dim)
        leading = lax.slice_in_dim(shard, 0, width, axis=dim)
        before = lax.ppermute(last, axis, up)
        after = lax.ppermute(leading, axis, down)
        shard = jnp.concatenate([before, shard, after], axis=dim)
    return shard


def from_root(block, axis, owner):
    block = jnp.where(lax.axis_index(axis) == owner, block, jnp.zeros_like(block))
    return lax.psum(block, axis)


def piece_of(field, axis_no, begin, extent):
    return lax.slice_in_dim(field, begin, begin + extent, axis=axis_no)


def pad_axis(field, axis_no):
    widths = [(0, 0)] * field.ndim
    widths[axis_no] = (2, 2)
    return jnp.pad(field, widths)


def second_diff(field, axis_no, extent):
    outer = piece_of(field, axis_no, 0, extent) + piece_of(field, axis_no, 4, extent)
    inner = piece_of(field, axis_no, 1, extent) + piece_of(field, axis_no, 3, extent)
    return (16.0 * inner - outer - 30.0 * piece_of(field, axis_no, 2, extent)) / 12.0


def first_diff(field, axis_no, extent):
    inner = piece_of(field, axis_no, 3, extent) - piece_of(field, axis_no, 1, extent)
    outer = piece_of(field, axis_no, 4, extent) - piece_of(field, axis_no, 0, extent)
    return (8.0 * inner - outer) / 12.0


def slopes(log_ext):
    width = log_ext.shape[0] - 4
    centre = piece_of(log_ext, 0, 2, width)
    wide_y = pad_axis(centre, 1)
    wide_z = pad_axis(centre, 2)
    return jnp.stack(
        [
            first_diff(log_ext, 0, width),
            first_diff(wide_y, 1, centre.shape[1]),
            first_diff(wide_z, 2, centre.shape[2]),
        ]
    )


def advance(field, before, courant, gradient):
    first_axis = field.ndim - 3
    width = field.shape[first_axis] - 4
    centre = piece_of(field, first_axis, 2, width)
    wide_y = pad_axis(centre, first_axis + 1)
    wide_z = pad_axis(centre, first_axis + 2)
    size_y = field.shape[first_axis + 1]
    size_z = field.shape[first_axis + 2]
    curvature = (
        second_diff(field, first_axis, width)
        + second_diff(wide_y, first_axis + 1, size_y)
        + second_diff(wide_z, first_axis + 2, size_z)
    )
    drift_term = (
        gradient[0] * first_diff(field, first_axis, width)
        + gradient[1] * first_diff(wide_y, first_axis + 1, size_y)
        + gradient[2] * first_diff(wide_z, first_axis + 2, size_z)
    )
    return 2.0 * centre - before + courant * (curvature + drift_term)


def local(
    adjoint_now,
    adjoint_before,
    courant_field,
    log_buoyancy,
    snapshot_store,
    owner_order,
    receiver_cells,
    receiver_traces,
    residual_weights,
):
    slab_rows = courant_field.shape[0]
    size_y = courant_field.shape[1]
    size_z = courant_field.shape[2]
    grid_rows = slab_rows * lax.axis_size("slab")
    row_anchor = lax.axis_index("slab") * slab_rows
    model_ext = extended(jnp.stack([courant_field, log_buoyancy]), (("slab", 1),), 4)
    courant_ext = model_ext[0, 2 : slab_rows + 6]
    gradient = slopes(model_ext[1])
    plane_ids = lax.broadcasted_iota(
        jnp.int32, (size_y, size_z), 0
    ) * size_z + lax.broadcasted_iota(jnp.int32, (size_y, size_z), 1)
    cell_column = receiver_cells[:, None, None, None]

    def evolve(field, before, offset, width, tick):
        upcoming = advance(
            field,
            before,
            courant_ext[offset - 2 : offset - 2 + width],
            gradient[:, offset - 2 : offset - 2 + width],
        )
        global_rows = row_anchor - 4 + offset + lax.broadcasted_iota(jnp.int32, (width,), 0)
        flat_ids = global_rows[:, None, None] * (size_y * size_z) + plane_ids[None]
        amplitude = receiver_traces[:, tick][:, None, None, None]
        upcoming = upcoming + jnp.where(flat_ids[None] == cell_column, amplitude, 0.0)
        return (upcoming, global_rows)

    current = adjoint_now
    previous = adjoint_before
    kernel_sum = jnp.zeros((slab_rows, size_y, size_z), jnp.float32)
    for snap_index in range(SNAPS):
        forward_field = from_root(snapshot_store[0], "rcv", owner_order[snap_index])
        current_ext = extended(current, (("slab", 1),), 4)
        previous_ext = extended(previous, (("slab", 1),), 2)
        middle, middle_rows = evolve(current_ext, previous_ext, 2, slab_rows + 4, 2 * snap_index)
        inside = (middle_rows >= 0) & (middle_rows < grid_rows)
        middle = jnp.where(inside[None, :, None, None], middle, 0.0)
        latest, unused_rows = evolve(middle, current, 4, slab_rows, 2 * snap_index + 1)
        previous = middle[:, 2 : slab_rows + 2]
        current = latest
        kernel_terms = jnp.sum(
            residual_weights[:, None, None, None] * current * forward_field, axis=0
        )
        kernel_sum = kernel_sum + kernel_terms
    sensitivity = lax.psum_scatter(kernel_sum, "rcv", scatter_dimension=1, tiled=True)
    return (sensitivity, current)


def solution(mesh):
    placed = (
        P("rcv", "slab", None, None),
        P("rcv", "slab", None, None),
        P("slab", None, None),
        P("slab", None, None),
        P("rcv", "slab", None, None),
        P(),
        P("rcv"),
        P("rcv", None),
        P("rcv"),
    )
    return jax.shard_map(
        local,
        mesh=mesh,
        in_specs=placed,
        out_specs=(P("slab", "rcv", None), P("rcv", "slab", None, None)),
        check_vma=False,
    )
```

profile of v0, /device:TPU:1, one launch (start us, length us, event | category | flops | bytes accessed | tf_op | source)
XLA Modules:
  0.0 783.1 jit_solution(6446867127906794386)
XLA Ops:
  7.2 0.0 copy-start.13
  7.2 0.0 all-reduce.25.cloned.1.call-start
  7.2 1.1 pad_maximum_fusion.8
  8.3 4.1 collective-permute-start.4
  12.4 1.3 collective-permute-start.5
  13.7 4.0 collective-permute-start
  17.7 1.3 collective-permute-start.1
  19.0 1.7 fusion.45
  20.7 4.6 collective-permute-start.2
  25.3 0.1 iota_add_fusion
  25.4 0.7 fusion.46
  26.8 1.3 collective-permute-start.3
  28.1 0.0 copy-start
  28.1 0.0 copy-start.9
  28.2 0.1 constant_dynamic-update-slice_fusion.1
  28.2 0.9 collective-permute-done.1
  29.2 0.0 copy-start.12
  29.3 0.1 pad_maximum_fusion
  29.5 0.6 copy-done.10
  30.1 0.2 copy-done.11
  30.3 4.7 collective-permute-done.3
  34.9 3.5 fusion.12
  38.4 0.0 copy-start.7
  38.5 0.0 copy-start.17
  38.5 2.0 fusion.37
  40.5 4.1 collective-permute-start.6
  44.6 1.3 collective-permute-start.7
  45.9 0.7 fusion.47
  49.2 0.0 copy-start.8
  49.2 1.0 fusion.44
  50.2 4.0 collective-permute-start.8
  54.2 1.3 collective-permute-start.9
  55.5 1.2 pad_maximum_fusion.1
  56.7 5.1 collective-permute-done.9
  61.8 2.9 fusion.15
  64.8 0.0 copy-start.15
  64.8 2.9 fusion.34
  67.6 4.3 collective-permute-start.10
  72.0 1.3 collective-permute-start.11
  73.3 1.0 broadcast_select_fusion.3
  74.3 0.0 all-reduce.25.cloned.1.call-update
  74.3 0.0 all-reduce.23.cloned.1.call-start
  74.4 1.0 fusion.43
  75.4 4.1 collective-permute-start.12
  79.5 1.3 collective-permute-start.13
  80.8 1.2 pad_maximum_fusion.2
  82.0 5.3 collective-permute-done.13
  87.3 3.0 fusion.18
  90.4 2.2 fusion.31
  92.5 4.2 collective-permute-start.14
  96.7 1.3 collective-permute-start.15
  98.7 4.6 collective-permute-start.16
  103.3 1.3 collective-permute-start.17
  104.6 0.1 pad_maximum_fusion.3
  104.7 1.8 collective-permute-done.16
  106.5 5.7 collective-permute-done.17
  112.2 1.8 fusion.21
  114.0 0.8 copy-done.3
  114.8 318.7 %all-reduce.25.cloned.1.call-done = (f32[1,4,128,128]{3,2,1,0:T(8,128)}, f32[1,4,128,128]{3,2,1,0:T(8,128)}, f32[1,4,128,128]{3,2,1,0:T(8,128)}, f32[1,4,128,128]{3,2,1,0:T(8,128)}) async-done(((f32[1,4,128,128]{3,2,1,0:T(8,128)}, f32[1,4,128,128]{3,2,1,0:T(8,128)}, f32[1,4,128,128]{3,2,1,0:T(8,128)}, f32[1,4,128,128]{3,2,1,0:T(8,128)}), (f32[1,4,128,128]{3,2,1,0:T(8,128)}, f32[1,4,128,128]{3,2,1,0:T(8,128)}, ...) | async-done | bytes 1048592 | tf_op jit(solution)/shard_map/psum | solution.py:24
  433.5 3.8 add_bitcast_fusion
  437.3 0.0 all-reduce.23.cloned.1.call-update
  437.3 1.3 dynamic-slice
  439.2 335.7 %all-reduce.23.cloned.1.call-done = f32[4,128,128]{2,1,0:T(8,128)} async-done(((f32[4,128,128]{2,1,0:T(8,128)}), f32[4,128,128]{2,1,0:T(8,128)}) %all-reduce.23.cloned.1.call-update) | async-done | bytes 262160
  774.9 1.3 constant_dynamic-slice_fusion
  (53 shorter events, 0.5 us)
Async XLA Ops:
  7.2 21.0 %copy-start.13 = (f32[1,4,128,128]{3,2,1,0:T(8,128)S(1)}, f32[1,4,128,128]{3,2,1,0:T(8,128)}, u32[]{:S(2)}) copy-start(f32[1,4,128,128]{3,2,1,0:T(8,128)} %param.9) | copy-start | bytes 786436
  7.2 18.2 %copy-start.16 = (f32[1,8]{1,0:T(1,128)S(1)}, f32[1,8]{1,0:T(1,128)}, u32[]{:S(2)}) copy-start(f32[1,8]{1,0:T(1,128)} %param.16) | copy-start | bytes 100
  7.2 426.3 %all-reduce.25.cloned.1.call-start = ((), (), s32[]{:S(2)}) async-start(), calls=%async_computation.1 | async-start | bytes 2097152 | tf_op jit(solution)/shard_map/psum | solution.py:24
  8.3 21.0 %collective-permute-start.4 = (f32[2,4,128,128]{3,2,1,0:T(8,128)S(1)}, f32[2,4,128,128]{3,2,1,0:T(8,128)S(1)}, u32[]{:S(2)}, u32[]{:S(2)}) collective-permute-start(f32[2,4,128,128]{3,2,1,0:T(8,128)S(1)} %pad_maximum_fusion.8), channel_id=1, source_target_pairs={{0,32},{32,64},{64,96},{96,128},{128,160},{160,192},{192,224},{224... | collective-permute-start | bytes 1572872 | tf_op jit(solution)/shard_map/ppermute | solution.py:16
  12.4 16.9 %collective-permute-start.5 = (f32[2,4,128,128]{3,2,1,0:T(8,128)S(1)}, f32[2,4,128,128]{3,2,1,0:T(8,128)S(1)}, u32[]{:S(2)}, u32[]{:S(2)}) collective-permute-start(f32[2,4,128,128]{3,2,1,0:T(8,128)S(1)} %pad_maximum_fusion.8), channel_id=1, source_target_pairs={{32,0},{64,32},{96,64},{128,96},{160,128},{192,160},{224,192},{256... | collective-permute-start | bytes 1572872 | tf_op jit(solution)/shard_map/ppermute | solution.py:17
  13.7 13.1 %collective-permute-start = (f32[1,4,128,128]{3,2,1,0:T(8,128)}, f32[1,4,128,128]{3,2,1,0:T(8,128)S(1)}, u32[]{:S(2)}, u32[]{:S(2)}) collective-permute-start(f32[1,4,128,128]{3,2,1,0:T(8,128)} %param.9), channel_id=1, source_target_pairs={{0,32},{32,64},{64,96},{96,128},{128,160},{160,192},{192,224},{224... | collective-permute-start | bytes 786440 | tf_op jit(solution)/shard_map/ppermute | solution.py:16
  17.7 11.5 %collective-permute-start.1 = (f32[1,4,128,128]{3,2,1,0:T(8,128)}, f32[1,4,128,128]{3,2,1,0:T(8,128)S(1)}, u32[]{:S(2)}, u32[]{:S(2)}) collective-permute-start(f32[1,4,128,128]{3,2,1,0:T(8,128)} %param.9), channel_id=1, source_target_pairs={{32,0},{64,32},{96,64},{128,96},{160,128},{192,160},{224,192},{256... | collective-permute-start | bytes 786440 | tf_op jit(solution)/shard_map/ppermute | solution.py:17
  20.7 9.6 %collective-permute-start.2 = (f32[1,2,128,128]{3,2,1,0:T(8,128)}, f32[1,2,128,128]{3,2,1,0:T(8,128)}, u32[]{:S(2)}, u32[]{:S(2)}) collective-permute-start(f32[1,2,128,128]{3,2,1,0:T(8,128)} %get-tuple-element.25), channel_id=1, source_target_pairs={{0,32},{32,64},{64,96},{96,128},{128,160},{160,192},{192,224},{224... | collective-permute-start | bytes 393224 | tf_op jit(solution)/shard_map/ppermute | solution.py:16
  26.8 8.2 %collective-permute-start.3 = (f32[1,2,128,128]{3,2,1,0:T(8,128)}, f32[1,2,128,128]{3,2,1,0:T(8,128)S(1)}, u32[]{:S(2)}, u32[]{:S(2)}) collective-permute-start(f32[1,2,128,128]{3,2,1,0:T(8,128)} %get-tuple-element.26), channel_id=1, source_target_pairs={{32,0},{64,32},{96,64},{128,96},{160,128},{192,160},{224,192},{256... | collective-permute-start | bytes 393224 | tf_op jit(solution)/shard_map/ppermute | solution.py:17
  28.1 1.2 copy-start
  28.1 1.2 copy-start.9
  29.2 5.7 copy-start.12
  29.3 0.8 copy-start.10
  29.3 1.0 copy-start.11
  34.9 3.5 copy-start.14
  38.4 2.1 copy-start.1
  38.4 6.2 copy-start.7
  38.5 7.4 copy-start.17
  40.5 15.0 %collective-permute-start.6 = (f32[1,4,128,128]{3,2,1,0:T(8,128)}, f32[1,4,128,128]{3,2,1,0:T(8,128)}, u32[]{:S(2)}, u32[]{:S(2)}) collective-permute-start(f32[1,4,128,128]{3,2,1,0:T(8,128)} %fusion.37), channel_id=1, source_target_pairs={{0,32},{32,64},{64,96},{96,128},{128,160},{160,192},{192,224},{224... | collective-permute-start | bytes 786440 | tf_op jit(solution)/shard_map/ppermute | solution.py:16
  44.6 10.9 %collective-permute-start.7 = (f32[1,4,128,128]{3,2,1,0:T(8,128)}, f32[1,4,128,128]{3,2,1,0:T(8,128)}, u32[]{:S(2)}, u32[]{:S(2)}) collective-permute-start(f32[1,4,128,128]{3,2,1,0:T(8,128)} %fusion.37), channel_id=1, source_target_pairs={{32,0},{64,32},{96,64},{128,96},{160,128},{192,160},{224,192},{256... | collective-permute-start | bytes 786440 | tf_op jit(solution)/shard_map/ppermute | solution.py:17
  49.2 12.7 %copy-start.8 = (f32[1,4,128,128]{3,2,1,0:T(8,128)S(1)}, f32[1,4,128,128]{3,2,1,0:T(8,128)}, u32[]{:S(2)}) copy-start(f32[1,4,128,128]{3,2,1,0:T(8,128)} %copy-done.7) | copy-start | bytes 786436
  50.2 6.5 collective-permute-start.8
  54.2 7.6 collective-permute-start.9
  64.7 2.9 copy-start.2
  64.8 9.5 %copy-start.5 = (f32[1,4,128,128]{3,2,1,0:T(8,128)}, f32[1,4,128,128]{3,2,1,0:T(8,128)S(1)}, u32[]{:S(2)}) copy-start(f32[1,4,128,128]{3,2,1,0:T(8,128)S(1)} %slice.739) | copy-start | bytes 786436
  64.8 8.5 %copy-start.15 = (f32[1,4,128,128]{3,2,1,0:T(8,128)S(1)}, f32[1,4,128,128]{3,2,1,0:T(8,128)}, u32[]{:S(2)}) copy-start(f32[1,4,128,128]{3,2,1,0:T(8,128)} %param.13) | copy-start | bytes 786436
  67.6 13.1 %collective-permute-start.10 = (f32[1,4,128,128]{3,2,1,0:T(8,128)}, f32[1,4,128,128]{3,2,1,0:T(8,128)}, u32[]{:S(2)}, u32[]{:S(2)}) collective-permute-start(f32[1,4,128,128]{3,2,1,0:T(8,128)} %fusion.34), channel_id=1, source_target_pairs={{0,32},{32,64},{64,96},{96,128},{128,160},{160,192},{192,224},{224... | collective-permute-start | bytes 786440 | tf_op jit(solution)/shard_map/ppermute | solution.py:16
  72.0 8.8 %collective-permute-start.11 = (f32[1,4,128,128]{3,2,1,0:T(8,128)}, f32[1,4,128,128]{3,2,1,0:T(8,128)}, u32[]{:S(2)}, u32[]{:S(2)}) collective-permute-start(f32[1,4,128,128]{3,2,1,0:T(8,128)} %fusion.34), channel_id=1, source_target_pairs={{32,0},{64,32},{96,64},{128,96},{160,128},{192,160},{224,192},{256... | collective-permute-start | bytes 786440 | tf_op jit(solution)/shard_map/ppermute | solution.py:17
  74.3 700.6 %all-reduce.23.cloned.1.call-start = ((), (), s32[]{:S(2)}) async-start(), calls=%async_computation | async-start | bytes 524288
  74.4 12.9 %copy-start.6 = (f32[1,4,128,128]{3,2,1,0:T(8,128)S(1)}, f32[1,4,128,128]{3,2,1,0:T(8,128)}, u32[]{:S(2)}) copy-start(f32[1,4,128,128]{3,2,1,0:T(8,128)} %copy-done.5) | copy-start | bytes 786436
  75.4 6.6 collective-permute-start.12
  79.5 7.8 collective-permute-start.13
  92.5 19.6 %copy-start.4 = (f32[1,4,128,128]{3,2,1,0:T(8,128)}, f32[1,4,128,128]{3,2,1,0:T(8,128)S(1)}, u32[]{:S(2)}) copy-start(f32[1,4,128,128]{3,2,1,0:T(8,128)S(1)} %fusion.31) | copy-start | bytes 786436
  92.5 12.0 %collective-permute-start.14 = (f32[1,4,128,128]{3,2,1,0:T(8,128)S(1)}, f32[1,4,128,128]{3,2,1,0:T(8,128)S(1)}, u32[]{:S(2)}, u32[]{:S(2)}) collective-permute-start(f32[1,4,128,128]{3,2,1,0:T(8,128)S(1)} %fusion.31), channel_id=1, source_target_pairs={{0,32},{32,64},{64,96},{96,128},{128,160},{160,192},{192,224},{224... | collective-permute-start | bytes 786440 | tf_op jit(solution)/shard_map/ppermute | solution.py:16
  96.7 7.9 %collective-permute-start.15 = (f32[1,4,128,128]{3,2,1,0:T(8,128)S(1)}, f32[1,4,128,128]{3,2,1,0:T(8,128)S(1)}, u32[]{:S(2)}, u32[]{:S(2)}) collective-permute-start(f32[1,4,128,128]{3,2,1,0:T(8,128)S(1)} %fusion.31), channel_id=1, source_target_pairs={{32,0},{64,32},{96,64},{128,96},{160,128},{192,160},{224,192},{256... | collective-permute-start | bytes 786440 | tf_op jit(solution)/shard_map/ppermute | solution.py:17
  98.7 7.8 collective-permute-start.16
  103.3 8.9 %collective-permute-start.17 = (f32[1,2,128,128]{3,2,1,0:T(8,128)S(1)}, f32[1,2,128,128]{3,2,1,0:T(8,128)S(1)}, u32[]{:S(2)}, u32[]{:S(2)}) collective-permute-start(f32[1,2,128,128]{3,2,1,0:T(8,128)S(1)} %get-tuple-element.13), channel_id=1, source_target_pairs={{32,0},{64,32},{96,64},{128,96},{160,128},{192,160},{224,192},{256... | collective-permute-start | bytes 393224 | tf_op jit(solution)/shard_map/ppermute | solution.py:17
  114.0 0.8 copy-start.3
Sparse Core Ops, SparseCore 0:
  74.4 359.0 all-reduce.24
  437.4 337.4 all-reduce.22
where the time goes:
time: 784 us; the launch traced here: 783 us
  waiting for transfers between devices  678 us (86%)
  starting transfers between devices  49.7 us (6%)
  other arithmetic  26.7 us (3%)
  between operations  19.1 us (2%)
  local copies, waits for them, and re-layouts  9.72 us (1%)
    unnamed x3, waiting for transfers between devices  336 us
    psum x1, waiting for transfers between devices, from_root(): return lax.psum(block, axis)  319 us
    ppermute x9, starting transfers between devices, extended(): before = lax.ppermute(last, axis, up)  38 us
    ppermute x9, waiting for transfers between devices, extended(): after = lax.ppermute(leading, axis, down)  21.6 us
  transfers between devices with their start and end apart: 20, of which 8 were waited for; matrix products, arithmetic and copies ran while one was open for 2% of the time, Pallas kernels for 0%

commit v1 on v0

--- a/solution.py
+++ b/solution.py
@@ -21,7 +21,7 @@
 
 def from_root(block, axis, owner):
     block = jnp.where(lax.axis_index(axis) == owner, block, jnp.zeros_like(block))
-    return lax.psum(block, axis)
+    return jnp.sum(lax.all_gather(block, axis), axis=0)
 
 
 def piece_of(field, axis_no, begin, extent):

time: 784 us -> 924 us (1.18)
  waiting for transfers between devices: 678 us -> 788 us
  starting transfers between devices: 49.7 us -> 70.6 us
    all_gather x0 -> x4, waiting for transfers between devices: none -> 445 us  [from_root(): return jnp.sum(lax.all_gather(block, axis), axis=0)]
    psum x1 -> x0, waiting for transfers between devices: 319 us -> none  [from_root(): return lax.psum(block, axis)]
    ppermute x9, starting transfers between devices: 38 us -> 58.8 us  [extended(): before = lax.ppermute(last, axis, up)]
    ppermute x9, waiting for transfers between devices: 21.6 us -> 3.06 us  [extended(): after = lax.ppermute(leading, axis, down)]
    reduce_sum x0 -> x4, other arithmetic: none -> 18.1 us  [from_root(): return jnp.sum(lax.all_gather(block, axis), axis=0)]
    unnamed x3 -> x6, waiting for transfers between devices: 336 us -> 337 us
  transfers between devices with their start and end apart: 20 -> 23, of which waited for: 8 -> 12; matrix products, arithmetic and copies ran while one was open for 2% -> 3% of each run, Pallas kernels for 0% -> 0%
where the time goes in v1:
time: 924 us; the launch traced here: 923 us
  waiting for transfers between devices  788 us (85%)
  starting transfers between devices  70.6 us (8%)
  other arithmetic  35.8 us (4%)
  between operations  18.8 us (2%)
  local copies, waits for them, and re-layouts  9.36 us (1%)
    all_gather x4, waiting for transfers between devices, from_root(): return jnp.sum(lax.all_gather(block, axis), axis=0)  445 us
    unnamed x6, waiting for transfers between devices  337 us
    ppermute x9, starting transfers between devices, extended(): before = lax.ppermute(last, axis, up)  58.8 us
  transfers between devices with their start and end apart: 23, of which 12 were waited for; matrix products, arithmetic and copies ran while one was open for 3% of the time, Pallas kernels for 0%

profile of v1, /device:TPU:1, one launch (start us, length us, event | category | flops | bytes accessed | tf_op | source)
XLA Modules:
  0.0 923.1 jit_solution(7897160453166045373)
XLA Ops:
  7.2 0.0 all-gather.11.cloned.1.call-start
  7.2 1.4 fusion.51
  11.2 2.0 broadcast_select_fusion.3
  13.2 0.0 all-gather.9.cloned.1.call-start
  13.2 0.7 all-gather.9.cloned.1.call-update
  14.0 0.7 all-gather.7.cloned.1.call-update
  14.7 0.5 all-gather.5.cloned.1.call-update
  15.3 4.0 collective-permute-start
  19.4 1.3 collective-permute-start.1
  20.7 1.3 collective-permute-start.5
  22.0 4.6 collective-permute-start.4
  26.7 0.7 fusion.49
  27.4 1.3 collective-permute-start.3
  28.7 0.7 fusion.50
  29.4 0.1 iota_add_fusion
  30.2 0.7 copy-done.8
  30.9 4.0 collective-permute-start.2
  34.9 1.0 constant_dynamic-update-slice_fusion.2
  35.9 0.1 constant_dynamic-update-slice_fusion.1
  36.0 1.0 constant_dynamic-update-slice_fusion
  37.1 0.1 pad_maximum_fusion
  37.2 0.7 copy-done.4
  37.9 0.2 copy-done.5
  38.1 0.9 collective-permute-done.3
  39.0 3.4 fusion.12
  42.4 1.2 fusion.41
  43.5 1.3 collective-permute-start.7
  44.8 7.0 collective-permute-start.6
  51.9 1.3 collective-permute-start.9
  53.2 4.0 collective-permute-start.8
  57.2 0.1 pad_maximum_fusion.1
  57.3 1.0 collective-permute-done.9
  58.3 1.1 collective-permute-done.8
  59.4 1.7 fusion.15
  61.2 1.2 fusion.38
  62.3 1.3 collective-permute-start.11
  63.6 16.5 %collective-permute-start.10 = (f32[1,4,128,128]{3,2,1,0:T(8,128)S(1)}, f32[1,4,128,128]{3,2,1,0:T(8,128)S(1)}, u32[]{:S(2)}, u32[]{:S(2)}) collective-permute-start(f32[1,4,128,128]{3,2,1,0:T(8,128)S(1)} %fusion.38), channel_id=1, source_target_pairs={{0,32},{32,64},{64,96},{96,128},{128,160},{160,192},{192,224},{224... | collective-permute-start | bytes 786440 | tf_op jit(solution)/shard_map/ppermute | solution.py:16
  80.1 1.3 collective-permute-start.13
  81.4 6.1 collective-permute-start.12
  87.6 0.1 pad_maximum_fusion.2
  87.7 0.7 collective-permute-done.13
  88.4 1.4 collective-permute-done.12
  89.7 1.8 fusion.18
  91.5 1.1 fusion.35
  92.6 1.3 collective-permute-start.15
  93.9 6.4 collective-permute-start.14
  101.0 1.3 collective-permute-start.17
  102.3 6.2 collective-permute-start.16
  108.5 0.1 pad_maximum_fusion.3
  108.6 0.5 collective-permute-done.17
  109.1 1.1 collective-permute-done.16
  110.2 1.8 fusion.21
  112.1 23.8 %all-gather.11.cloned.1.call-done = f32[32,4,128,128]{3,2,1,0:T(8,128)} async-done(((f32[1,4,128,128]{3,2,1,0:T(8,128)}), f32[32,4,128,128]{3,2,1,0:T(8,128)}) %all-gather.11.cloned.1.call-update) | async-done | bytes 8388624 | tf_op jit(solution)/shard_map/all_gather | solution.py:24
  135.8 4.5 reduce_sum.41
  140.4 161.5 %all-gather.9.cloned.1.call-done = f32[32,4,128,128]{3,2,1,0:T(8,128)} async-done(((f32[1,4,128,128]{3,2,1,0:T(8,128)}), f32[32,4,128,128]{3,2,1,0:T(8,128)}) %all-gather.9.cloned.1.call-update) | async-done | bytes 8388624 | tf_op jit(solution)/shard_map/all_gather | solution.py:24
  301.8 4.5 reduce_sum.37
  306.4 129.5 %all-gather.7.cloned.1.call-done = f32[32,4,128,128]{3,2,1,0:T(8,128)} async-done(((f32[1,4,128,128]{3,2,1,0:T(8,128)}), f32[32,4,128,128]{3,2,1,0:T(8,128)}) %all-gather.7.cloned.1.call-update) | async-done | bytes 8388624 | tf_op jit(solution)/shard_map/all_gather | solution.py:24
  435.9 4.5 reduce_sum.36
  440.4 130.0 %all-gather.5.cloned.1.call-done = f32[32,4,128,128]{3,2,1,0:T(8,128)} async-done(((f32[1,4,128,128]{3,2,1,0:T(8,128)}), f32[32,4,128,128]{3,2,1,0:T(8,128)}) %all-gather.5.cloned.1.call-update) | async-done | bytes 8388624 | tf_op jit(solution)/shard_map/all_gather | solution.py:24
  570.3 4.5 reduce_sum.35
  574.9 3.3 fusion.27
  578.2 1.3 dynamic-slice
  580.1 335.2 %all-reduce.21.cloned.1.call-done = f32[4,128,128]{2,1,0:T(8,128)} async-done(((f32[4,128,128]{2,1,0:T(8,128)}), f32[4,128,128]{2,1,0:T(8,128)}) %all-reduce.21.cloned.1.call-update) | async-done | bytes 262160
  915.3 1.3 constant_dynamic-slice_fusion
  (51 shorter events, 0.6 us)
Async XLA Ops:
  7.2 8.1 copy-start.7
  7.2 13.5 %copy-start.3 = (f32[4,128,128]{2,1,0:T(8,128)S(1)}, f32[4,128,128]{2,1,0:T(8,128)}, u32[]{:S(2)}) copy-start(f32[4,128,128]{2,1,0:T(8,128)} %param.12) | copy-start | bytes 786436
  7.2 13.5 %copy-start = (f32[4,128,128]{2,1,0:T(8,128)S(1)}, f32[4,128,128]{2,1,0:T(8,128)}, u32[]{:S(2)}) copy-start(f32[4,128,128]{2,1,0:T(8,128)} %param.11) | copy-start | bytes 786436
  7.2 128.6 %all-gather.11.cloned.1.call-start = ((), (), s32[]{:S(2)}) async-start(), calls=%async_computation.3 | async-start | bytes 8650752 | tf_op jit(solution)/shard_map/all_gather | solution.py:24
  11.2 15.5 %copy-start.6 = (f32[1,4,128,128]{3,2,1,0:T(8,128)S(1)}, f32[1,4,128,128]{3,2,1,0:T(8,128)}, u32[]{:S(2)}) copy-start(f32[1,4,128,128]{3,2,1,0:T(8,128)} %param.10) | copy-start | bytes 786436
  13.2 15.6 %copy-start.9 = (f32[1,8]{1,0:T(1,128)S(1)}, f32[1,8]{1,0:T(1,128)}, u32[]{:S(2)}) copy-start(f32[1,8]{1,0:T(1,128)} %param.16) | copy-start | bytes 100
  13.2 288.6 %all-gather.9.cloned.1.call-start = ((), (), s32[]{:S(2)}) async-start(), calls=%async_computation.2 | async-start | bytes 8650752 | tf_op jit(solution)/shard_map/all_gather | solution.py:24
  13.9 421.9 %all-gather.7.cloned.1.call-start = ((), (), s32[]{:S(2)}) async-start(), calls=%async_computation.1 | async-start | bytes 8650752 | tf_op jit(solution)/shard_map/all_gather | solution.py:24
  14.7 555.7 %all-gather.5.cloned.1.call-start = ((), (), s32[]{:S(2)}) async-start(), calls=%async_computation | async-start | bytes 8650752 | tf_op jit(solution)/shard_map/all_gather | solution.py:24
  15.2 900.0 %all-reduce.21.cloned.1.call-start = ((), (), s32[]{:S(2)}) async-start(), calls=%async_computation.4 | async-start | bytes 524288
  15.3 14.9 %collective-permute-start = (f32[1,4,128,128]{3,2,1,0:T(8,128)S(1)}, f32[1,4,128,128]{3,2,1,0:T(8,128)S(1)}, u32[]{:S(2)}, u32[]{:S(2)}) collective-permute-start(f32[1,4,128,128]{3,2,1,0:T(8,128)S(1)} %copy-done.7), channel_id=1, source_target_pairs={{0,32},{32,64},{64,96},{96,128},{128,160},{160,192},{192,224},{224... | collective-permute-start | bytes 786440 | tf_op jit(solution)/shard_map/ppermute | solution.py:16
  19.4 16.6 %collective-permute-start.1 = (f32[1,4,128,128]{3,2,1,0:T(8,128)S(1)}, f32[1,4,128,128]{3,2,1,0:T(8,128)}, u32[]{:S(2)}, u32[]{:S(2)}) collective-permute-start(f32[1,4,128,128]{3,2,1,0:T(8,128)S(1)} %copy-done.7), channel_id=1, source_target_pairs={{32,0},{64,32},{96,64},{128,96},{160,128},{192,160},{224,192},{256... | collective-permute-start | bytes 786440 | tf_op jit(solution)/shard_map/ppermute | solution.py:17
  20.7 16.3 %collective-permute-start.5 = (f32[2,4,128,128]{3,2,1,0:T(8,128)S(1)}, f32[2,4,128,128]{3,2,1,0:T(8,128)S(1)}, u32[]{:S(2)}, u32[]{:S(2)}) collective-permute-start(f32[2,4,128,128]{3,2,1,0:T(8,128)S(1)} %pad_maximum_fusion.8), channel_id=1, source_target_pairs={{32,0},{64,32},{96,64},{128,96},{160,128},{192,160},{224,192},{256... | collective-permute-start | bytes 1572872 | tf_op jit(solution)/shard_map/ppermute | solution.py:17
  22.0 15.0 %collective-permute-start.4 = (f32[2,4,128,128]{3,2,1,0:T(8,128)S(1)}, f32[2,4,128,128]{3,2,1,0:T(8,128)S(1)}, u32[]{:S(2)}, u32[]{:S(2)}) collective-permute-start(f32[2,4,128,128]{3,2,1,0:T(8,128)S(1)} %pad_maximum_fusion.8), channel_id=1, source_target_pairs={{0,32},{32,64},{64,96},{96,128},{128,160},{160,192},{192,224},{224... | collective-permute-start | bytes 1572872 | tf_op jit(solution)/shard_map/ppermute | solution.py:16
  27.4 11.5 %collective-permute-start.3 = (f32[1,2,128,128]{3,2,1,0:T(8,128)}, f32[1,2,128,128]{3,2,1,0:T(8,128)}, u32[]{:S(2)}, u32[]{:S(2)}) collective-permute-start(f32[1,2,128,128]{3,2,1,0:T(8,128)} %get-tuple-element.22), channel_id=1, source_target_pairs={{32,0},{64,32},{96,64},{128,96},{160,128},{192,160},{224,192},{256... | collective-permute-start | bytes 393224 | tf_op jit(solution)/shard_map/ppermute | solution.py:17
  30.2 0.7 copy-start.8
  30.9 8.0 collective-permute-start.2
  37.0 0.8 copy-start.4
  37.0 1.0 copy-start.5
  43.5 13.7 %collective-permute-start.7 = (f32[1,4,128,128]{3,2,1,0:T(8,128)S(1)}, f32[1,4,128,128]{3,2,1,0:T(8,128)S(1)}, u32[]{:S(2)}, u32[]{:S(2)}) collective-permute-start(f32[1,4,128,128]{3,2,1,0:T(8,128)S(1)} %fusion.41), channel_id=1, source_target_pairs={{32,0},{64,32},{96,64},{128,96},{160,128},{192,160},{224,192},{256... | collective-permute-start | bytes 786440 | tf_op jit(solution)/shard_map/ppermute | solution.py:17
  44.8 12.4 %collective-permute-start.6 = (f32[1,4,128,128]{3,2,1,0:T(8,128)S(1)}, f32[1,4,128,128]{3,2,1,0:T(8,128)S(1)}, u32[]{:S(2)}, u32[]{:S(2)}) collective-permute-start(f32[1,4,128,128]{3,2,1,0:T(8,128)S(1)} %fusion.41), channel_id=1, source_target_pairs={{0,32},{32,64},{64,96},{96,128},{128,160},{160,192},{192,224},{224... | collective-permute-start | bytes 786440 | tf_op jit(solution)/shard_map/ppermute | solution.py:16
  51.9 6.4 collective-permute-start.9
  53.2 6.2 collective-permute-start.8
  62.3 25.2 %collective-permute-start.11 = (f32[1,4,128,128]{3,2,1,0:T(8,128)S(1)}, f32[1,4,128,128]{3,2,1,0:T(8,128)S(1)}, u32[]{:S(2)}, u32[]{:S(2)}) collective-permute-start(f32[1,4,128,128]{3,2,1,0:T(8,128)S(1)} %fusion.38), channel_id=1, source_target_pairs={{32,0},{64,32},{96,64},{128,96},{160,128},{192,160},{224,192},{256... | collective-permute-start | bytes 786440 | tf_op jit(solution)/shard_map/ppermute | solution.py:17
  63.6 23.9 %collective-permute-start.10 = (f32[1,4,128,128]{3,2,1,0:T(8,128)S(1)}, f32[1,4,128,128]{3,2,1,0:T(8,128)S(1)}, u32[]{:S(2)}, u32[]{:S(2)}) collective-permute-start(f32[1,4,128,128]{3,2,1,0:T(8,128)S(1)} %fusion.38), channel_id=1, source_target_pairs={{0,32},{32,64},{64,96},{96,128},{128,160},{160,192},{192,224},{224... | collective-permute-start | bytes 786440 | tf_op jit(solution)/shard_map/ppermute | solution.py:16
  80.1 8.2 collective-permute-start.13
  81.4 8.3 collective-permute-start.12
  92.6 15.8 %collective-permute-start.15 = (f32[1,4,128,128]{3,2,1,0:T(8,128)S(1)}, f32[1,4,128,128]{3,2,1,0:T(8,128)S(1)}, u32[]{:S(2)}, u32[]{:S(2)}) collective-permute-start(f32[1,4,128,128]{3,2,1,0:T(8,128)S(1)} %fusion.35), channel_id=1, source_target_pairs={{32,0},{64,32},{96,64},{128,96},{160,128},{192,160},{224,192},{256... | collective-permute-start | bytes 786440 | tf_op jit(solution)/shard_map/ppermute | solution.py:17
  93.9 14.6 %collective-permute-start.14 = (f32[1,4,128,128]{3,2,1,0:T(8,128)S(1)}, f32[1,4,128,128]{3,2,1,0:T(8,128)S(1)}, u32[]{:S(2)}, u32[]{:S(2)}) collective-permute-start(f32[1,4,128,128]{3,2,1,0:T(8,128)S(1)} %fusion.35), channel_id=1, source_target_pairs={{0,32},{32,64},{64,96},{96,128},{128,160},{160,192},{192,224},{224... | collective-permute-start | bytes 786440 | tf_op jit(solution)/shard_map/ppermute | solution.py:16
  101.0 8.1 collective-permute-start.17
  102.3 7.9 collective-permute-start.16
  112.1 28.3 %copy-start.1 = (f32[1,8,128,128]{3,2,1,0:T(8,128)}, f32[1,8,128,128]{3,2,1,0:T(8,128)S(1)}, u32[]{:S(2)}) copy-start(f32[1,8,128,128]{3,2,1,0:T(8,128)S(1)} %fusion.21) | copy-start | bytes 1572868
  440.4 134.5 %copy-start.2 = (f32[1,8,128,128]{3,2,1,0:T(8,128)S(1)}, f32[1,8,128,128]{3,2,1,0:T(8,128)}, u32[]{:S(2)}) copy-start(f32[1,8,128,128]{3,2,1,0:T(8,128)} %copy-done.1) | copy-start | bytes 1572868
  440.4 134.5 %slice-start = ((f32[1,8,128,128]{3,2,1,0:T(8,128)}), f32[1,4,128,128]{3,2,1,0:T(8,128)S(1)}, s32[]{:S(2)}) async-start(f32[1,8,128,128]{3,2,1,0:T(8,128)} %copy-done.1), calls=%async_computation.5 | async-start | bytes 524288 | tf_op jit(solution)/shard_map/slice | solution.py:28
Sparse Core Ops, SparseCore 0:
  13.3 122.4 all-gather.10
  139.0 162.8 all-gather.8
  305.0 130.8 all-gather.6
  439.4 130.8 all-gather.4
  578.3 336.9 all-reduce.20
